TPU v7x, 256 devices: a whole 4x4x8 slice. The times are simulated.
256 devices in a mesh: seq: 16 (over y, z_lo, core), row: 4 (over z_hi), col: 4 (over x).
Axes of the slice: x: 4, y: 4, z: 8 (z_hi: 4, z_lo: 2; z = z_hi * 2 + z_lo), core: 2. Of those that a mesh axis runs over, the one named last changes fastest.
Arguments:
- tokens: bfloat16 [8192, 4096], P(('seq', 'row'), 'col'), may hold values from -6 to 6
- w_uvqk: bfloat16 [4096, 8192], P(('seq', 'row'), 'col'), may hold values from -0.09375 to 0.09375
- w_out: bfloat16 [2048, 4096], P('col', ('seq', 'row')), may hold values from -0.375 to 0.375
- rab_table: float32 [16, 32], replicated, may hold values from -4 to 4
- norm_gain: float32 [16, 128], replicated, may hold values from 0.5 to 2
- user_lengths: int32 [4], replicated, may hold values from 1 to 6144, 8192 in all
- bucket_ids: int32 [8192], P('seq'), may hold values from 0 to 8191, as said below
Outputs:
- layer_out: bfloat16 [8192, 4096], P(('seq', 'row'), 'col')
Inputs may be any that keep to these rules, and one draw needn't show every extreme that they name: bucket_ids never fall from one token to the next.
All inputs are finite; a program needn't handle non-finite values.
Results may differ from a plain program's by a relative error of at most 0.014.
Values may be sent and summed in bfloat16 or wider, within the bound.
No kernel may reach another device: no remote copies, remote signals or barrier semaphores. Data moves between devices by JAX's collectives and lax.ppermute only.
A program may use at most 64 MiB of HBM per device.

v0:
```python
import math
import jax
import jax.numpy as jnp
from jax import lax
from jax.sharding import PartitionSpec as P

DH = 128
NB = 32
norm_eps = 1e-05


def user_index(user_ends, positions):
    return jnp.sum((user_ends[None, :] <= positions[:, None]).astype(jnp.int32), axis=1)


def bucket_biases(table_rows, bucket_gap):
    one_hot = (bucket_gap[:, :, None] == jnp.arange(NB, dtype=jnp.int32)[None, None, :]).astype(
        jnp.float32
    )
    return jnp.einsum(
        "qkb,hb->hqk",
        one_hot,
        table_rows,
        precision=lax.Precision.HIGHEST,
        preferred_element_type=jnp.float32,
    )


def on_device(tokens, w_uvqk, w_out, rab_table, norm_gain, user_lengths, bucket_ids):
    feature_rows = lax.all_gather(tokens, "col", axis=1, tiled=True)
    local_rows = tokens.shape[0]
    width_cols = w_uvqk.shape[1]
    row_index = lax.axis_index("row")
    col_index = lax.axis_index("col")
    seq_index = lax.axis_index("seq")
    projected = jnp.dot(
        feature_rows,
        lax.all_gather(w_uvqk, ("seq", "row"), axis=0, tiled=True),
        preferred_element_type=jnp.float32,
    )
    local_heads = width_cols // (4 * DH)
    activated = jax.nn.silu(projected).astype(jnp.bfloat16).reshape(local_rows, local_heads, 4, DH)
    head_major = lax.all_to_all(activated, "row", split_axis=1, concat_axis=0, tiled=True)
    block_len = head_major.shape[0]
    per_device = head_major.shape[1]
    user_ends = jnp.cumsum(user_lengths)
    query_pos = seq_index * block_len + jnp.arange(block_len, dtype=jnp.int32)
    query_user = user_index(user_ends, query_pos)
    first_head = col_index * local_heads + row_index * per_device
    rab_rows = lax.dynamic_slice_in_dim(rab_table, first_head, per_device, 0)
    gain_rows = lax.dynamic_slice_in_dim(norm_gain, first_head, per_device, 0)
    queries = head_major[:, :, 2]
    key_value = head_major[:, :, 1:4:2]
    score_scale = DH ** (-0.5)
    running = jnp.zeros((block_len, per_device, DH), jnp.float32)
    kv_piece = lax.all_gather(key_value, "seq", axis=0, tiled=True)
    key_bucket = lax.all_gather(bucket_ids, "seq", axis=0, tiled=True)
    key_count = kv_piece.shape[0]
    sub_size = math.gcd(key_count, 256)
    sub_count = key_count // sub_size

    def sub_block(accum_in, sub_index):
        sub_first = sub_index * sub_size
        kv_sub = lax.dynamic_slice_in_dim(kv_piece, sub_first, sub_size, 0)
        bucket_sub = lax.dynamic_slice_in_dim(key_bucket, sub_first, sub_size, 0)
        key_pos = sub_first + jnp.arange(sub_size, dtype=jnp.int32)
        key_user = user_index(user_ends, key_pos)
        visible = (query_user[:, None] == key_user[None, :]) & (
            key_pos[None, :] <= query_pos[:, None]
        )
        bucket_gap = jnp.clip(bucket_ids[:, None] - bucket_sub[None, :], 0, NB - 1)
        biases = bucket_biases(rab_rows, bucket_gap)
        scores = (
            jnp.dot(queries[:, 0], kv_sub[:, 0, 1].T, preferred_element_type=jnp.float32)
            * score_scale
        )
        scores = scores + biases[0]
        weights = jnp.where(visible, jax.nn.silu(scores), jnp.float32(0.0)).astype(jnp.bfloat16)
        per_head = [jnp.dot(weights, kv_sub[:, 0, 0], preferred_element_type=jnp.float32)]
        accum_out = accum_in + jnp.stack(per_head, axis=1)
        return (accum_out, None)

    running, _ = lax.scan(sub_block, running, jnp.arange(sub_count, dtype=jnp.int32))
    head_mean = jnp.mean(running, axis=-1, keepdims=True)
    centered = running - head_mean
    head_var = jnp.mean(centered * centered, axis=-1, keepdims=True)
    normed = centered * lax.rsqrt(head_var + norm_eps) * gain_rows[None, :, :]
    gated = (normed * head_major[:, :, 0].astype(jnp.float32)).astype(jnp.bfloat16)
    token_major = lax.all_to_all(gated, "row", split_axis=0, concat_axis=1, tiled=True)
    gated_rows = token_major.reshape(local_rows, local_heads * DH)
    partials = jnp.dot(
        gated_rows,
        lax.all_gather(w_out, ("seq", "row"), axis=1, tiled=True),
        preferred_element_type=jnp.float32,
    )
    summed = lax.psum_scatter(
        partials.astype(jnp.bfloat16), "col", scatter_dimension=1, tiled=True
    ).astype(jnp.float32)
    return (tokens.astype(jnp.float32) + summed).astype(jnp.bfloat16)


def solution(mesh):
    placed = (
        P(("seq", "row"), "col"),
        P(("seq", "row"), "col"),
        P("col", ("seq", "row")),
        P(),
        P(),
        P(),
        P("seq"),
    )
    return jax.shard_map(
        on_device, mesh=mesh, in_specs=placed, out_specs=P(("seq", "row"), "col"), check_vma=False
    )
```

profile of v0, /device:TPU:8, one launch (start us, length us, event | category | flops | bytes accessed | tf_op | source)
XLA Modules:
  0.0 657.6 jit_solution(16882960967085766931)
XLA Ops:
  8.1 30.5 %all-gather.6.cloned.1.call-done = bf16[128,4096]{1,0:T(8,128)(2,1)} async-done(((bf16[128,1024]{1,0:T(8,128)(2,1)}), bf16[128,4096]{1,0:T(8,128)(2,1)}) %all-gather.6.cloned.1.call-update) | async-done | bytes 1048592 | tf_op jit(solution)/shard_map/all_gather | solution.py:30
  38.6 203.7 %all-gather.8.cloned.1.call-done = bf16[4096,2048]{1,0:T(8,128)(2,1)} async-done(((bf16[64,2048]{1,0:T(8,128)(2,1)}), bf16[4096,2048]{1,0:T(8,128)(2,1)}) %all-gather.8.cloned.1.call-update) | async-done | bytes 16777232 | tf_op jit(solution)/shard_map/all_gather | solution.py:38
  242.3 8.5 %multiply_convert_fusion = bf16[128,2048]{1,0:T(8,128)(2,1)S(1)} fusion(bf16[128,4096]{1,0:T(8,128)(2,1)} %all-gather.6.cloned.1.call-done, bf16[4096,2048]{1,0:T(8,128)(2,1)} %all-gather.8.cloned.1.call-done), kind=kOutput, calls=%fused_computation.33 | convolution fusion | flops 2148794368 | bytes 18350080 | tf_op jit(solution)/shard_map/dot_general | solution.py:36
  251.4 27.6 %all_to_all.33 = bf16[128,4,4,128]{3,2,0,1:T(4,128)(2,1)S(1)} all-to-all(bf16[128,4,4,128]{3,2,0,1:T(4,128)(2,1)S(1)} %copy.26), channel_id=1, replica_groups=mesh['seq'=16,'row'=4,'col'=4] {'row'}, dimensions={1} | all-to-all | bytes 1048576 | tf_op jit(solution)/shard_map/all_to_all | solution.py:43
  280.7 14.5 %all-gather = s32[16,1,512]{2,1,0:T(1,128)S(1)} all-gather(s32[1,1,512]{2,1,0:T(1,128)S(1)} %bitcast.80), channel_id=1, replica_groups=mesh['seq'=16,'row'=4,'col'=4] {'seq'}, dimensions={0}, use_global_device_ids=true | all-gather | bytes 34816 | tf_op jit(solution)/shard_map/all_gather | solution.py:57
  296.0 19.7 %all-gather.10.cloned.1.call-done = bf16[8192,1,2,128]{3,0,2,1:T(8,128)(2,1)} async-done(((bf16[512,1,2,128]{3,0,2,1:T(8,128)(2,1)}), bf16[8192,1,2,128]{3,0,2,1:T(8,128)(2,1)}) %all-gather.10.cloned.1.call-update) | async-done | bytes 4194320 | tf_op jit(solution)/shard_map/all_gather | solution.py:56
  315.8 289.0 %while.11 = (s32[]{:T(128)}, f32[512,1,128]{2,0,1:T(8,128)S(1)}, s32[512]{0:T(512)S(1)}, s32[4]{0:T(128)S(1)}, s32[32]{0:T(128)S(1)}, /*index=5*/bf16[8192,1,2,1...) while((s32[]{:T(128)}, f32[512,1,128]{2,0,1:T(8,128)S(1)}, ...), condition=%wide.region_4.5_spmd.clone, body=%wide.region_2.4_spmd.clone.sunk | while | flops 123473408 | bytes 3950976 | solution.py:83
  317.2 5.3 fusion.36
  326.3 5.3 fusion.36
  335.3 5.3 fusion.36
  341.3 1.5 fusion.37
  344.3 5.3 fusion.36
  353.4 5.3 fusion.36
  362.4 5.3 fusion.36
  368.4 1.5 fusion.37
  371.4 5.3 fusion.36
  377.5 1.5 fusion.37
  380.5 5.3 fusion.36
  389.5 5.3 fusion.36
  398.5 5.3 fusion.36
  407.6 5.3 fusion.36
  416.6 5.3 fusion.36
  422.6 1.5 fusion.37
  425.6 5.3 fusion.36
  434.6 5.3 fusion.36
  443.7 5.3 fusion.36
  449.7 1.5 fusion.37
  452.7 5.3 fusion.36
  461.7 5.3 fusion.36
  470.8 5.3 fusion.36
  479.8 5.3 fusion.36
  488.8 5.3 fusion.36
  497.9 5.3 fusion.36
  506.9 5.3 fusion.36
  515.9 5.3 fusion.36
  525.0 5.3 fusion.36
  534.0 5.3 fusion.36
  543.0 5.3 fusion.36
  552.1 5.3 fusion.36
  561.1 5.3 fusion.36
  570.1 5.3 fusion.36
  579.2 5.3 fusion.36
  588.2 5.3 fusion.36
  597.2 5.3 fusion.36
  606.6 15.3 %all_to_all.34 = bf16[4,2,8192]{2,1,0:T(2,128)(2,1)S(1)} all-to-all(bf16[4,2,8192]{2,1,0:T(2,128)(2,1)S(1)} %reshape.130), channel_id=1, replica_groups=mesh['seq'=16,'row'=4,'col'=4] {'row'}, dimensions={0} | all-to-all | bytes 262144 | tf_op jit(solution)/shard_map/all_to_all | solution.py:89
  622.3 4.7 convolution_convert_fusion
  627.0 22.4 %reduce-scatter.2.cloned.1.call-done = bf16[128,1024]{1,0:T(8,128)(2,1)} async-done(((bf16[128,4096]{1,0:T(8,128)(2,1)}), bf16[128,1024]{1,0:T(8,128)(2,1)}) %reduce-scatter.2.cloned.1.call-update) | async-done | bytes 262160 | tf_op jit(solution)/shard_map/reduce_scatter | solution.py:96
  649.4 1.7 add_convert_fusion
  (293 shorter events, 97.2 us)
Async XLA Ops:
  6.5 289.4 %copy-start = (f32[16,128]{1,0:T(8,128)S(1)}, f32[16,128]{1,0:T(8,128)}, u32[]{:S(2)}) copy-start(f32[16,128]{1,0:T(8,128)} %param.13) | copy-start | bytes 24580
  6.5 32.0 %all-gather.6.cloned.1.call-start = ((), (), s32[]{:S(2)}) async-start(), calls=%async_computation.3 | async-start | bytes 1310720 | tf_op jit(solution)/shard_map/all_gather | solution.py:30
  7.3 235.0 %all-gather.8.cloned.1.call-start = ((), (), s32[]{:S(2)}) async-start(), calls=%async_computation.4 | async-start | bytes 17039360 | tf_op jit(solution)/shard_map/all_gather | solution.py:38
  8.0 307.7 %all-gather.10.cloned.1.call-start = ((), (), s32[]{:S(2)}) async-start(), calls=%async_computation.5 | async-start | bytes 4456448 | tf_op jit(solution)/shard_map/all_gather | solution.py:56
  250.8 29.7 %copy-start.3 = (s32[4]{0:T(128)S(1)}, s32[4]{0:T(128)}, u32[]{:S(2)}) copy-start(s32[4]{0:T(128)} %param.14) | copy-start | bytes 52
  250.8 29.9 %copy-start.2 = (s32[512]{0:T(512)S(1)}, s32[512]{0:T(512)}, u32[]{:S(2)}) copy-start(s32[512]{0:T(512)} %param.15) | copy-start | bytes 6148
  279.9 342.4 %all-gather.12.cloned.1.call-start = ((), (), s32[]{:S(2)}) async-start(), calls=%async_computation.6 | async-start | bytes 4259840 | tf_op jit(solution)/shard_map/all_gather | solution.py:93
  280.5 368.9 %reduce-scatter.2.cloned.1.call-start = ((), (), s32[]{:S(2)}) async-start(), calls=%async_computation.7 | async-start | bytes 1310720 | tf_op jit(solution)/shard_map/reduce_scatter | solution.py:96
  605.4 44.0 %copy-start.1 = (bf16[128,1024]{1,0:T(8,128)(2,1)S(1)}, bf16[128,1024]{1,0:T(8,128)(2,1)}, u32[]{:S(2)}) copy-start(bf16[128,1024]{1,0:T(8,128)(2,1)} %param.9) | copy-start | bytes 786436
Sparse Core Ops, SparseCore 0:
  9.2 29.3 all-gather.5
  40.4 201.8 all-gather.7
  280.0 35.7 all-gather.9
  317.4 185.4 all-gather.11
  627.1 22.2 reduce-scatter.1
where the time goes:
time: 660 us; the launch traced here: 658 us
  waiting for transfers between devices  278 us (42%)
  matrix products  229 us (35%)
  blocking collectives  57.5 us (9%)
  local copies, waits for them, and re-layouts  45.7 us (7%)
  loops' own time  22.8 us (3%)
  between operations  13.3 us (2%)
  other arithmetic  11.2 us (2%)
    all_gather x1, waiting for transfers between devices, on_device(): lax.all_gather(w_uvqk, ('seq', 'row'), axis=0, tiled=True)  204 us
    dot_general x32, matrix products, bucket_biases(): jnp.einsum('qkb,hb->hqk', one_hot, table_rows, precision=lax.Precision.HI...  168 us
    dot_general x32, matrix products, sub_block(): jnp.dot(weights, kv_sub[:, 0, 0], preferred_element_type=jnp.float32)  47.3 us
    all_gather x1, waiting for transfers between devices, on_device(): feature_rows = lax.all_gather(tokens, 'col', axis=1, tiled=True)  30.5 us
    all_to_all x1, blocking collectives, on_device(): lax.all_to_all(activated, 'row', split_axis=1, concat_axis=0, tiled=True)  27.6 us
    another operation x1, loops' own time, on_device(): lax.scan(sub_block, running, jnp.arange(sub_count, dtype=jnp.int32))  22.8 us
    reduce_scatter x1, waiting for transfers between devices, on_device(): lax.psum_scatter(partials.astype(jnp.bfloat16), 'col', scatter_dimension=...  22.4 us
    dot_general x32, local copies, waits for them, and re-layouts, bucket_biases(): jnp.einsum('qkb,hb->hqk', one_hot, table_rows, precision=lax.Precision.HI...  21.5 us
  transfers between devices with their start and end apart: 5, of which 4 were waited for; matrix products, arithmetic and copies ran while one was open for 41% of the time, Pallas kernels for 0%

commit v1 on v0

--- a/solution.py
+++ b/solution.py
@@ -7,6 +7,27 @@
 DH = 128
 NB = 32
 norm_eps = 1e-05
+
+
+def gather_around(x, axis, dim):
+    length, here, rows = (lax.axis_size(axis), lax.axis_index(axis), x.shape[dim])
+    right = [(i, (i + 1) % length) for i in range(length)]
+    behind = [(i, (i - 1) % length) for i in range(length)]
+    filled = jnp.zeros((*x.shape[:dim], length * rows, *x.shape[dim + 1 :]), x.dtype)
+    filled = lax.dynamic_update_slice_in_dim(filled, x, here * rows, axis=dim)
+    from_left = from_right = x
+    halfway = length // 2
+    for turn in range(1, halfway + 1):
+        from_left = lax.ppermute(from_left, axis, right)
+        filled = lax.dynamic_update_slice_in_dim(
+            filled, from_left, (here - turn) % length * rows, axis=dim
+        )
+        if turn < length - halfway:
+            from_right = lax.ppermute(from_right, axis, behind)
+            filled = lax.dynamic_update_slice_in_dim(
+                filled, from_right, (here + turn) % length * rows, axis=dim
+            )
+    return filled
 
 
 def user_index(user_ends, positions):
@@ -27,7 +48,7 @@
 
 
 def on_device(tokens, w_uvqk, w_out, rab_table, norm_gain, user_lengths, bucket_ids):
-    feature_rows = lax.all_gather(tokens, "col", axis=1, tiled=True)
+    feature_rows = gather_around(tokens, "col", 1)
     local_rows = tokens.shape[0]
     width_cols = w_uvqk.shape[1]
     row_index = lax.axis_index("row")

time: 660 us -> 630 us (0.955)
  waiting for transfers between devices: 278 us -> 244 us
    all_gather x1 -> x0, waiting for transfers between devices: 30.5 us -> none  [on_device(): feature_rows = lax.all_gather(tokens, 'col', axis=1, tiled=True)]
    all_gather x1, waiting for transfers between devices: 204 us -> 188 us  [on_device(): lax.all_gather(w_uvqk, ('seq', 'row'), axis=0, tiled=True)]
    ppermute x0 -> x3, waiting for transfers between devices: none -> 13.1 us  [the longest x2 13.1 us: gather_around(): from_left = lax.ppermute(from_left, axis, right)]
  transfers between devices with their start and end apart: 5 -> 7, of which waited for: 4 -> 5; matrix products, arithmetic and copies ran while one was open for 41% -> 43% of each run, Pallas kernels for 0% -> 0%
where the time goes in v1:
time: 630 us; the launch traced here: 628 us
  waiting for transfers between devices  244 us (39%)
  matrix products  228 us (36%)
  blocking collectives  57.7 us (9%)
  local copies, waits for them, and re-layouts  46.8 us (7%)
  loops' own time  22.8 us (4%)
  between operations  13.4 us (2%)
  other arithmetic  11.2 us (2%)
    all_gather x1, waiting for transfers between devices, on_device(): lax.all_gather(w_uvqk, ('seq', 'row'), axis=0, tiled=True)  188 us
    dot_general x32, matrix products, bucket_biases(): jnp.einsum('qkb,hb->hqk', one_hot, table_rows, precision=lax.Precision.HI...  168 us
    dot_general x32, matrix products, sub_block(): jnp.dot(weights, kv_sub[:, 0, 0], preferred_element_type=jnp.float32)  47.2 us
    all_to_all x1, blocking collectives, on_device(): lax.all_to_all(activated, 'row', split_axis=1, concat_axis=0, tiled=True)  27.6 us
    another operation x1, loops' own time, on_device(): lax.scan(sub_block, running, jnp.arange(sub_count, dtype=jnp.int32))  22.8 us
    reduce_scatter x1, waiting for transfers between devices, on_device(): lax.psum_scatter(partials.astype(jnp.bfloat16), 'col', scatter_dimension=...  22 us
    dot_general x32, local copies, waits for them, and re-layouts, bucket_biases(): jnp.einsum('qkb,hb->hqk', one_hot, table_rows, precision=lax.Precision.HI...  21.5 us
    all_gather x1, waiting for transfers between devices, on_device(): kv_piece = lax.all_gather(key_value, 'seq', axis=0, tiled=True)  19.4 us
  transfers between devices with their start and end apart: 7, of which 5 were waited for; matrix products, arithmetic and copies ran while one was open for 43% of the time, Pallas kernels for 0%

profile of v1, /device:TPU:8, one launch (start us, length us, event | category | flops | bytes accessed | tf_op | source)
XLA Modules:
  0.0 628.3 jit_solution(17029313743916248028)
XLA Ops:
  7.3 1.6 collective-permute-start
  8.9 1.7 collective-permute-start.1
  10.6 6.2 collective-permute-done
  18.3 6.9 %collective-permute-done.2 = bf16[128,1024]{1,0:T(8,128)(2,1)S(1)} collective-permute-done((bf16[128,1024]{1,0:T(8,128)(2,1)S(1)}, bf16[128,1024]{1,0:T(8,128)(2,1)S(1)}, u32[]{:S(2)}, u32[]{:S(2)}) %collective-permute-start.2) | collective-permute-done | bytes 262176 | tf_op jit(solution)/shard_map/ppermute | solution.py:21
  25.3 188.3 %all-gather.5.cloned.1.call-done = bf16[4096,2048]{1,0:T(8,128)(2,1)} async-done(((bf16[64,2048]{1,0:T(8,128)(2,1)}), bf16[4096,2048]{1,0:T(8,128)(2,1)}) %all-gather.5.cloned.1.call-update) | async-done | bytes 16777232 | tf_op jit(solution)/shard_map/all_gather | solution.py:59
  213.6 8.2 %multiply_convert_fusion = bf16[128,2048]{1,0:T(8,128)(2,1)S(1)} fusion(bf16[128,4096]{1,0:T(8,128)(2,1)S(1)} %constant_dynamic-update-slice_fusion, bf16[4096,2048]{1,0:T(8,128)(2,1)} %all-gather.5.cloned.1.call-done), kind=kOutput, calls=%fused_computation.33 | convolution fusion | flops 2148794368 | bytes 18350080 | tf_op jit(solution)/shard_map/dot_general | solution.py:57
  222.4 27.6 %all_to_all.33 = bf16[128,4,4,128]{3,2,0,1:T(4,128)(2,1)S(1)} all-to-all(bf16[128,4,4,128]{3,2,0,1:T(4,128)(2,1)S(1)} %copy.26), channel_id=1, replica_groups=mesh['seq'=16,'row'=4,'col'=4] {'row'}, dimensions={1} | all-to-all | bytes 1048576 | tf_op jit(solution)/shard_map/all_to_all | solution.py:64
  251.9 14.6 %all-gather = s32[16,1,512]{2,1,0:T(1,128)S(1)} all-gather(s32[1,1,512]{2,1,0:T(1,128)S(1)} %bitcast.80), channel_id=1, replica_groups=mesh['seq'=16,'row'=4,'col'=4] {'seq'}, dimensions={0}, use_global_device_ids=true | all-gather | bytes 34816 | tf_op jit(solution)/shard_map/all_gather | solution.py:78
  267.4 19.4 %all-gather.7.cloned.1.call-done = bf16[8192,1,2,128]{3,0,2,1:T(8,128)(2,1)} async-done(((bf16[512,1,2,128]{3,0,2,1:T(8,128)(2,1)}), bf16[8192,1,2,128]{3,0,2,1:T(8,128)(2,1)}) %all-gather.7.cloned.1.call-update) | async-done | bytes 4194320 | tf_op jit(solution)/shard_map/all_gather | solution.py:77
  286.8 288.9 %while.11 = (s32[]{:T(128)}, f32[512,1,128]{2,0,1:T(8,128)S(1)}, s32[512]{0:T(512)S(1)}, s32[4]{0:T(128)S(1)}, s32[32]{0:T(128)S(1)}, /*index=5*/bf16[8192,1,2,1...) while((s32[]{:T(128)}, f32[512,1,128]{2,0,1:T(8,128)S(1)}, ...), condition=%wide.region_4.5_spmd.clone, body=%wide.region_2.4_spmd.clone.sunk | while | flops 123473408 | bytes 3950976 | solution.py:104
  288.3 5.3 fusion.37
  297.3 5.3 fusion.37
  306.3 5.3 fusion.37
  315.4 5.3 fusion.37
  324.4 5.3 fusion.37
  333.4 5.3 fusion.37
  339.5 1.5 fusion.38
  342.5 5.3 fusion.37
  351.5 5.3 fusion.37
  360.5 5.3 fusion.37
  366.6 1.5 fusion.38
  369.5 5.3 fusion.37
  378.6 5.3 fusion.37
  387.6 5.3 fusion.37
  396.6 5.3 fusion.37
  405.7 5.3 fusion.37
  414.7 5.3 fusion.37
  423.7 5.3 fusion.37
  432.7 5.3 fusion.37
  441.8 5.3 fusion.37
  450.8 5.3 fusion.37
  459.8 5.3 fusion.37
  468.9 5.3 fusion.37
  477.9 5.3 fusion.37
  486.9 5.3 fusion.37
  495.9 5.3 fusion.37
  505.0 5.3 fusion.37
  514.0 5.3 fusion.37
  523.0 5.3 fusion.37
  532.1 5.3 fusion.37
  541.1 5.3 fusion.37
  550.1 5.3 fusion.37
  559.1 5.3 fusion.37
  568.2 5.3 fusion.37
  577.6 15.4 %all_to_all.34 = bf16[4,2,8192]{2,1,0:T(2,128)(2,1)S(1)} all-to-all(bf16[4,2,8192]{2,1,0:T(2,128)(2,1)S(1)} %reshape.130), channel_id=1, replica_groups=mesh['seq'=16,'row'=4,'col'=4] {'row'}, dimensions={0} | all-to-all | bytes 262144 | tf_op jit(solution)/shard_map/all_to_all | solution.py:110
  593.3 4.7 convolution_convert_fusion
  598.0 22.0 %reduce-scatter.2.cloned.1.call-done = bf16[128,1024]{1,0:T(8,128)(2,1)} async-done(((bf16[128,4096]{1,0:T(8,128)(2,1)}), bf16[128,1024]{1,0:T(8,128)(2,1)}) %reduce-scatter.2.cloned.1.call-update) | async-done | bytes 262160 | tf_op jit(solution)/shard_map/reduce_scatter | solution.py:117
  620.0 1.7 add_convert_fusion
  (301 shorter events, 102.4 us)
Async XLA Ops:
  6.5 260.7 %copy-start = (f32[16,128]{1,0:T(8,128)S(1)}, f32[16,128]{1,0:T(8,128)}, u32[]{:S(2)}) copy-start(f32[16,128]{1,0:T(8,128)} %param.13) | copy-start | bytes 24580
  6.5 207.0 %all-gather.5.cloned.1.call-start = ((), (), s32[]{:S(2)}) async-start(), calls=%async_computation.3 | async-start | bytes 17039360 | tf_op jit(solution)/shard_map/all_gather | solution.py:59
  7.3 279.5 %all-gather.7.cloned.1.call-start = ((), (), s32[]{:S(2)}) async-start(), calls=%async_computation.4 | async-start | bytes 4456448 | tf_op jit(solution)/shard_map/all_gather | solution.py:77
  7.3 9.5 %collective-permute-start = (bf16[128,1024]{1,0:T(8,128)(2,1)}, bf16[128,1024]{1,0:T(8,128)(2,1)S(1)}, u32[]{:S(2)}, u32[]{:S(2)}) collective-permute-start(bf16[128,1024]{1,0:T(8,128)(2,1)} %param.9), channel_id=1, source_target_pairs={{0,1},{1,2},{2,3},{3,0},{4,5},{5,6},{6,7},{7,4},{8,9},{9,10},{10,1... | collective-permute-start | bytes 786440 | tf_op jit(solution)/shard_map/ppermute | solution.py:21
  8.9 9.4 %collective-permute-start.1 = (bf16[128,1024]{1,0:T(8,128)(2,1)}, bf16[128,1024]{1,0:T(8,128)(2,1)S(1)}, u32[]{:S(2)}, u32[]{:S(2)}) collective-permute-start(bf16[128,1024]{1,0:T(8,128)(2,1)} %param.9), channel_id=1, source_target_pairs={{0,3},{1,0},{2,1},{3,2},{4,7},{5,4},{6,5},{7,6},{8,11},{9,8},{10,9... | collective-permute-start | bytes 786440 | tf_op jit(solution)/shard_map/ppermute | solution.py:26
  16.8 8.4 %collective-permute-start.2 = (bf16[128,1024]{1,0:T(8,128)(2,1)S(1)}, bf16[128,1024]{1,0:T(8,128)(2,1)S(1)}, u32[]{:S(2)}, u32[]{:S(2)}) collective-permute-start(bf16[128,1024]{1,0:T(8,128)(2,1)S(1)} %collective-permute-done), channel_id=1, source_target_pairs={{0,1},{1,2},{2,3},{3,0},{4,5},{5,6},{6,7},{7,4},{8,9},{9,10},{10,1... | collective-permute-start | bytes 786440 | tf_op jit(solution)/shard_map/ppermute | solution.py:21
  221.8 29.9 %copy-start.3 = (s32[4]{0:T(128)S(1)}, s32[4]{0:T(128)}, u32[]{:S(2)}) copy-start(s32[4]{0:T(128)} %param.14) | copy-start | bytes 52
  221.8 30.1 %copy-start.2 = (s32[512]{0:T(512)S(1)}, s32[512]{0:T(512)}, u32[]{:S(2)}) copy-start(s32[512]{0:T(512)} %param.15) | copy-start | bytes 6148
  250.9 342.4 %all-gather.9.cloned.1.call-start = ((), (), s32[]{:S(2)}) async-start(), calls=%async_computation.5 | async-start | bytes 4259840 | tf_op jit(solution)/shard_map/all_gather | solution.py:114
  251.7 368.3 %reduce-scatter.2.cloned.1.call-start = ((), (), s32[]{:S(2)}) async-start(), calls=%async_computation.6 | async-start | bytes 1310720 | tf_op jit(solution)/shard_map/reduce_scatter | solution.py:117
  576.3 43.7 %copy-start.1 = (bf16[128,1024]{1,0:T(8,128)(2,1)S(1)}, bf16[128,1024]{1,0:T(8,128)(2,1)}, u32[]{:S(2)}) copy-start(bf16[128,1024]{1,0:T(8,128)(2,1)} %param.9) | copy-start | bytes 786436
Sparse Core Ops, SparseCore 0:
  9.2 204.3 all-gather.4
  251.0 35.7 all-gather.6
  288.6 185.3 all-gather.8
  598.1 21.8 reduce-scatter.1
